TPU v7x, 256 devices: a whole 4x4x8 slice. The times are simulated.
256 devices in a mesh: user: 32 (over z, x), tp: 8 (over y, core).
Axes of the slice: x: 4, y: 4, z: 8, core: 2. Of those that a mesh axis runs over, the one named last changes fastest.
Arguments:
- cand_feats: bfloat16 [32768, 1024], P('user', 'tp'), may hold values from -6 to 6
- w_in: bfloat16 [1024, 2048], P(None, 'tp'), may hold values from -0.1875 to 0.1875
- w_out: bfloat16 [1024, 1024], P('tp'), may hold values from -0.1875 to 0.1875
- kv_cache: bfloat16 [2048, 128, 2048], P('user', None, 'tp'), may hold values from -6 to 6
- event_mask: int32 [2048, 128], P('user'), may hold values from 0 to 1, as said below
- block_counts: int32 [256], P('user'), may hold values from 1 to 8, as said below
- user_blocks: int32 [256, 8], P('user'), may hold values from 0 to 63, as said below
- send_slots: int32 [1024, 2], P('user'), may hold values from 0 to 63, as said below
- cand_user: int32 [32768], P('user'), may hold values from 0 to 7
Outputs:
- scored: bfloat16 [32768, 1024], P('user', 'tp')
Inputs may be any that keep to these rules, and one draw needn't show every extreme that they name: `block_counts`: on every index of the user axis some user has 8 blocks, and on one index every user has. For user u of the index r of the user axis and j < block_counts[r * 8 + u], user_blocks[r * 8 + u, j] = o * 2 + c says that block j of u's history is cached on index o, in its local row send_slots[o * 32 + r, c] of kv_cache and event_mask. These valid entries of one index's users are all different, and on one index they take all 64 values. Entries with j >= block_counts[u] are arbitrary. `send_slots`: the 32 rows of one holder o (rows o * 32 to o * 32 + 31) name each of its local rows 0 to 63 exactly once. `event_mask`: in every block of a user's history the first event is real.
All inputs are finite; a program needn't handle non-finite values.
Results may differ from a plain program's by a relative error of at most 0.013.
Values may be sent and summed in bfloat16 or wider, within the bound.
A program may use at most 128 MiB of HBM per device.

v0:
```python
import jax
import jax.numpy as jnp
from jax import lax
from jax.sharding import PartitionSpec as P

DH = 128
EVENTS = 128
norm_eps = 1e-06


def owner_users(block_count, block_table, slot_count):
    user_count, most_blocks = block_table.shape
    live_mask = jnp.arange(most_blocks, dtype=jnp.int32)[None, :] < block_count[:, None]
    slot_hit = (
        block_table[:, :, None] == jnp.arange(slot_count, dtype=jnp.int32)[None, None, :]
    ) & live_mask[:, :, None]
    user_label = jnp.arange(user_count, dtype=jnp.int32)[:, None, None] + 1
    return jnp.sum(jnp.where(slot_hit, user_label, 0), axis=(0, 1)) - 1


def attend(queries, users, key_pairs, marks, owners):
    row_count, heads_here = (queries.shape[0], queries.shape[1])
    block_rows = min(512, row_count)
    pair_rows = key_pairs.reshape(-1, heads_here, 2, DH)
    key_rows = pair_rows[:, :, 0, :]
    value_rows = pair_rows[:, :, 1, :]
    live_mask = marks.reshape(-1, EVENTS).astype(jnp.float32)
    owner_label = owners.astype(jnp.float32)

    def one_block(packed):
        query_block, user_block = packed
        same_user = (user_block.astype(jnp.float32)[:, None] == owner_label[None, :]).astype(
            jnp.float32
        )
        weights = (same_user[:, :, None] * live_mask[None]).reshape(query_block.shape[0], -1)
        scores = jnp.einsum(
            "rhd,ehd->hre", query_block, key_rows, preferred_element_type=jnp.float32
        ) * DH ** (-0.5)
        attn_weights = (jax.nn.silu(scores) * weights[None]).astype(jnp.bfloat16)
        return jnp.einsum(
            "hre,ehd->rhd", attn_weights, value_rows, preferred_element_type=jnp.float32
        )

    result = lax.map(
        one_block, (queries.reshape(-1, block_rows, heads_here, DH), users.reshape(-1, block_rows))
    )
    return result.reshape(row_count, heads_here, DH)


def per_device(
    cand_feats, w_in, w_out, kv_cache, event_mask, block_counts, user_blocks, send_slots, cand_user
):
    row_count = cand_feats.shape[0]
    heads_here = w_out.shape[0] // DH
    projected = jnp.dot(
        lax.all_gather(cand_feats, "tp", axis=1, tiled=True),
        w_in,
        preferred_element_type=jnp.float32,
    )
    activated = jax.nn.silu(projected).reshape(row_count, heads_here, 2, DH)
    queries = activated[:, :, 0, :].astype(jnp.bfloat16)
    gates = activated[:, :, 1, :].astype(jnp.bfloat16)
    peer_count = lax.axis_size("user")
    capacity = send_slots.shape[1]
    slot_users = owner_users(block_counts, user_blocks, peer_count * capacity)
    picked = send_slots.reshape(-1)
    outgoing = kv_cache[picked].reshape(peer_count, capacity, EVENTS, kv_cache.shape[2])
    out_marks = event_mask[picked].reshape(peer_count, capacity, EVENTS).astype(jnp.bfloat16)
    arrived, arrived_marks = (
        lax.all_to_all(outgoing, "user", split_axis=0, concat_axis=0, tiled=True),
        lax.all_to_all(out_marks, "user", split_axis=0, concat_axis=0, tiled=True),
    )
    attended = attend(queries, cand_user, arrived, arrived_marks, slot_users)
    normed = (
        attended
        * lax.rsqrt(jnp.mean(attended * attended, axis=-1, keepdims=True) + norm_eps)
        * gates.astype(jnp.float32)
    )
    hidden = normed.astype(jnp.bfloat16).reshape(row_count, heads_here * DH)
    head_terms = jnp.dot(hidden, w_out, preferred_element_type=jnp.float32)
    summed = lax.psum_scatter(
        head_terms.astype(jnp.bfloat16), "tp", scatter_dimension=1, tiled=True
    ).astype(jnp.float32)
    return (cand_feats.astype(jnp.float32) + summed).astype(jnp.bfloat16)


def solution(mesh):
    in_specs = (
        P("user", "tp"),
        P(None, "tp"),
        P("tp", None),
        P("user", None, "tp"),
        P("user", None),
        P("user"),
        P("user", None),
        P("user", None),
        P("user"),
    )
    out_specs = P("user", "tp")
    return jax.shard_map(
        per_device, mesh=mesh, in_specs=in_specs, out_specs=out_specs, check_vma=False
    )
```

profile of v0, /device:TPU:2, one launch (start us, length us, event | category | flops | bytes accessed | tf_op | source)
XLA Modules:
  0.0 248.5 jit_solution(2677720347667687180)
XLA Ops:
  6.5 0.8 copy.22
  7.5 1.4 gather_fusion.1
  9.5 11.6 %all-to-all-start.1 = ((bf16[32,2,128]{2,1,0:T(2,128)(2,1)}), bf16[32,2,128]{2,1,0:T(2,128)(2,1)S(1)}, u32[]{:S(2)}, u32[]{:S(2)}) async-start(bf16[32,2,128]{2,1,0:T(2,128)(2,1)} %bitcast.14), calls=%async_computation.1 | async-start | bytes 32768 | tf_op jit(solution)/shard_map/all_to_all | solution.py:71
  21.1 5.0 %gather_fusion = bf16[64,128,256]{2,1,0:T(8,128)(2,1)} fusion(bf16[64,128,256]{2,1,0:T(8,128)(2,1)} %param.14, s32[1024]{0:T(1024)S(1)} %pad_clamp_fusion), kind=kCustom, calls=%fused_computation | custom fusion | bytes 8388864 | tf_op jit(solution)/shard_map/gather | solution.py:67
  26.0 3.5 %all-to-all-done.1 = bf16[32,2,128]{2,1,0:T(2,128)(2,1)S(1)} async-done(((bf16[32,2,128]{2,1,0:T(2,128)(2,1)}), bf16[32,2,128]{2,1,0:T(2,128)(2,1)S(1)}, u32[]{:S(2)}, u32[]{:S(2)}) %all-to-all-start.1) | async-done | bytes 16416 | tf_op jit(solution)/shard_map/all_to_all | solution.py:71
  29.5 6.5 %all-to-all-start = ((bf16[32,2,128,256]{3,2,1,0:T(8,128)(2,1)}), bf16[32,2,128,256]{3,2,1,0:T(8,128)(2,1)}, u32[]{:S(2)}, u32[]{:S(2)}) async-start(bf16[32,2,128,256]{3,2,1,0:T(8,128)(2,1)} %bitcast.92), calls=%async_computation | async-start | bytes 8388608 | tf_op jit(solution)/shard_map/all_to_all | solution.py:70
  37.1 32.6 %all-gather.2.cloned.1.call-done = bf16[1024,1024]{1,0:T(8,128)(2,1)} async-done(((bf16[1024,128]{1,0:T(8,128)(2,1)}), bf16[1024,1024]{1,0:T(8,128)(2,1)}) %all-gather.2.cloned.1.call-update) | async-done | bytes 2097168 | tf_op jit(solution)/shard_map/all_gather | solution.py:56
  69.7 2.5 %multiply_convert_fusion = bf16[1024,256]{0,1:T(8,128)(2,1)S(1)} fusion(bf16[1024,1024]{1,0:T(8,128)(2,1)} %all-gather.2.cloned.1.call-done, bf16[1024,256]{1,0:T(8,128)(2,1)S(1)} %copy-done), kind=kOutput, calls=%fused_computation.20 | convolution fusion | flops 538181632 | bytes 3145728 | tf_op jit(solution)/shard_map/dot_general | solution.py:55
  72.2 0.8 copy-done.2
  73.0 0.8 copy.29
  73.8 55.0 %all-to-all-done = bf16[32,2,128,256]{3,2,1,0:T(8,128)(2,1)} async-done(((bf16[32,2,128,256]{3,2,1,0:T(8,128)(2,1)}), bf16[32,2,128,256]{3,2,1,0:T(8,128)(2,1)}, u32[]{:S(2)}, u32[]{:S(2)}) %all-to-all-start) | async-done | bytes 4194336 | tf_op jit(solution)/shard_map/all_to_all | solution.py:70
  128.9 7.0 %reshape.203 = bf16[8192,1,2,128]{3,2,0,1:T(2,128)(2,1)} reshape(bf16[32,2,128,256]{3,2,1,0:T(8,128)(2,1)} %all-to-all-done) | data formatting | bytes 8388608 | tf_op jit(solution)/shard_map/reshape | solution.py:24
  135.8 8.9 %fusion.29 = (bf16[8192,1,1,128]{3,2,0,1:T(2,128)(2,1)S(1)}, bf16[8192,1,1,128]{3,2,0,1:T(2,128)(2,1)S(1)}) fusion(bf16[8192,1,2,128]{3,2,0,1:T(2,128)(2,1)} %reshape.203), kind=kLoop, calls=%fused_computation.37 | loop fusion | bytes 8388608 | tf_op jit(solution)/shard_map/slice | solution.py:26
  144.7 1.9 copy_bitcast_fusion
  146.6 53.2 %while.10 = (s32[]{:T(128)}, f32[2,512,1,128]{3,1,2,0:T(8,128)S(1)}, bf16[2,512,1,128]{3,1,2,0:T(8,128)(2,1)}, bf16[8192,1,128]{2,0,1:T(8,128)(2,1)}, s32[2,512]...) while((s32[]{:T(128)}, ...), condition=%wide.region_2.3_spmd, body=%wide.region_1.2_spmd.sunk | while | flops 2181104128 | bytes 38444384 | solution.py:44
  146.8 7.0 %mul.127 = f32[512,64,128]{2,1,0:T(8,128)} broadcast(f32[512,64]{1,0:T(8,128)S(1)} %compare_convert_fusion.2), dimensions={0,1} | broadcast | bytes 16908288 | tf_op jit(solution)/shard_map/while/body/eval_jaxpr/mul | solution.py:35
  153.8 19.4 %fusion.40 = f32[2,512,1,128]{3,1,2,0:T(8,128)S(1)} fusion(f32[2,512,1,128]{3,1,2,0:T(8,128)S(1)} %get-tuple-element.151, s32[]{:T(128)} %get-tuple-element.150, bf16[8192,1,128]{2,0,1:T(8,128)(2,1)S(1)} %get-tuple-element.166, f32[64,8,64,128]{3,2,1,0:T(8,128)} %bitcast.91, f32[8192]{0:T(1024)S(1)} %bitcast.101, ...), kind=kOutput, calls=%fused_computation.9.clone.1 | convolution fusion | flops 2181038080 | bytes 21398528 | tf_op jit(solution)/shard_map/while/body/eval_jaxpr/hre,ehd->rhd/dot_general | solution.py:40
  173.4 7.0 %mul.127 = f32[512,64,128]{2,1,0:T(8,128)} broadcast(f32[512,64]{1,0:T(8,128)S(1)} %compare_convert_fusion.2), dimensions={0,1} | broadcast | bytes 16908288 | tf_op jit(solution)/shard_map/while/body/eval_jaxpr/mul | solution.py:35
  180.4 19.4 %fusion.40 = f32[2,512,1,128]{3,1,2,0:T(8,128)S(1)} fusion(f32[2,512,1,128]{3,1,2,0:T(8,128)S(1)} %get-tuple-element.151, s32[]{:T(128)} %get-tuple-element.150, bf16[8192,1,128]{2,0,1:T(8,128)(2,1)S(1)} %get-tuple-element.166, f32[64,8,64,128]{3,2,1,0:T(8,128)} %bitcast.91, f32[8192]{0:T(1024)S(1)} %bitcast.101, ...), kind=kOutput, calls=%fused_computation.9.clone.1 | convolution fusion | flops 2181038080 | bytes 21398528 | tf_op jit(solution)/shard_map/while/body/eval_jaxpr/hre,ehd->rhd/dot_general | solution.py:40
  200.3 1.7 convolution_convert_fusion
  202.0 2.6 %copy.25 = bf16[1024,1024]{0,1:T(8,128)(2,1)} copy(bf16[1024,1024]{1,0:T(8,128)(2,1)S(1)} %convolution_convert_fusion) | data formatting | bytes 4194304
  204.6 35.1 %reduce-scatter.4.cloned.1.call-done = bf16[128,1024]{1,0:T(8,128)(2,1)} async-done(((bf16[1024,1024]{1,0:T(8,128)(2,1)}), bf16[128,1024]{1,0:T(8,128)(2,1)}) %reduce-scatter.4.cloned.1.call-update) | async-done | bytes 262160
  239.8 1.1 copy.26
  240.9 0.8 add_convert_fusion
  (37 shorter events, 2.5 us)
Async XLA Ops:
  6.5 63.1 %copy-start = (bf16[1024,256]{1,0:T(8,128)(2,1)S(1)}, bf16[1024,256]{1,0:T(8,128)(2,1)}, u32[]{:S(2)}) copy-start(bf16[1024,256]{1,0:T(8,128)(2,1)} %param.12) | copy-start | bytes 1572868
  9.5 20.1 %all-to-all-start.1 = ((bf16[32,2,128]{2,1,0:T(2,128)(2,1)}), bf16[32,2,128]{2,1,0:T(2,128)(2,1)S(1)}, u32[]{:S(2)}, u32[]{:S(2)}) async-start(bf16[32,2,128]{2,1,0:T(2,128)(2,1)} %bitcast.14), calls=%async_computation.1 | async-start | bytes 32768 | tf_op jit(solution)/shard_map/all_to_all | solution.py:71
  29.5 7.3 %copy-start.5 = (s32[1024]{0:T(1024)S(1)}, s32[1024]{0:T(1024)}, u32[]{:S(2)}) copy-start(s32[1024]{0:T(1024)} %param.19) | copy-start | bytes 12292
  29.5 7.3 %copy-start.6 = (s32[8]{0:T(128)S(1)}, s32[8]{0:T(128)}, u32[]{:S(2)}) copy-start(s32[8]{0:T(128)} %param.16) | copy-start | bytes 100
  29.5 7.4 %copy-start.4 = (s32[8,8]{1,0:T(8,128)S(1)}, s32[8,8]{1,0:T(8,128)}, u32[]{:S(2)}) copy-start(s32[8,8]{1,0:T(8,128)} %param.17) | copy-start | bytes 772
  29.5 99.3 %all-to-all-start = ((bf16[32,2,128,256]{3,2,1,0:T(8,128)(2,1)}), bf16[32,2,128,256]{3,2,1,0:T(8,128)(2,1)}, u32[]{:S(2)}, u32[]{:S(2)}) async-start(bf16[32,2,128,256]{3,2,1,0:T(8,128)(2,1)} %bitcast.92), calls=%async_computation | async-start | bytes 8388608 | tf_op jit(solution)/shard_map/all_to_all | solution.py:70
  36.0 33.6 %all-gather.2.cloned.1.call-start = ((), (), s32[]{:S(2)}) async-start(), calls=%async_computation.3 | async-start | bytes 2359296 | tf_op jit(solution)/shard_map/all_gather | solution.py:56
  36.8 203.0 %reduce-scatter.4.cloned.1.call-start = ((), (), s32[]{:S(2)}) async-start(), calls=%async_computation.4 | async-start | bytes 2359296
  72.2 0.8 copy-start.2
  146.6 53.7 %copy-start.3 = (bf16[128,1024]{1,0:T(8,128)(2,1)S(1)}, bf16[128,1024]{1,0:T(8,128)(2,1)}, u32[]{:S(2)}) copy-start(bf16[128,1024]{1,0:T(8,128)(2,1)} %param.13) | copy-start | bytes 786436
  202.0 38.9 %copy-start.1 = (bf16[1024,128]{1,0:T(8,128)(2,1)S(1)}, bf16[1024,128]{1,0:T(8,128)(2,1)}, u32[]{:S(2)}) copy-start(bf16[1024,128]{1,0:T(8,128)(2,1)} %param.11) | copy-start | bytes 786436
Sparse Core Ops, SparseCore 0:
  38.7 30.9 all-gather.1
  204.7 34.9 reduce-scatter.3
where the time goes:
time: 249 us
  waiting for transfers between devices  127 us (51%)
  local copies, waits for them, and re-layouts  44.6 us (18%)
  matrix products  43 us (17%)
  starting transfers between devices  18.2 us (7%)
  between operations  13.6 us (5%)
    all_to_all x1, waiting for transfers between devices, per_device(): lax.all_to_all(outgoing, 'user', split_axis=0, concat_axis=0, tiled=True)  55 us
    dot_general x2, matrix products, one_block(): jnp.einsum('hre,ehd->rhd', attn_weights, value_rows, preferred_element_ty...  38.9 us
    unnamed x3, waiting for transfers between devices  35.8 us
    all_gather x1, waiting for transfers between devices, per_device(): lax.all_gather(cand_feats, 'tp', axis=1, tiled=True)  32.6 us
    mul x2, local copies, waits for them, and re-layouts, one_block(): same_user[:, :, None] * live_mask[None]  14 us
    all_to_all x1, starting transfers between devices, per_device(): lax.all_to_all(out_marks, 'user', split_axis=0, concat_axis=0, tiled=True)  11.6 us
    slice x1, local copies, waits for them, and re-layouts, attend(): value_rows = pair_rows[:, :, 1, :]  8.89 us
    unnamed x20, local copies, waits for them, and re-layouts  8.03 us
  transfers between devices with their start and end apart: 4, of which 4 were waited for; matrix products, arithmetic and copies ran while one was open for 3% of the time, Pallas kernels for 0%

commit v1 on v0

--- a/solution.py
+++ b/solution.py
@@ -6,6 +6,19 @@
 DH = 128
 EVENTS = 128
 norm_eps = 1e-06
+
+
+def collect(array, axis, dim):
+    ways = lax.axis_size(axis)
+    up = [(d, (d + 1) % ways) for d in range(ways)]
+    down = [(d, (d - 1) % ways) for d in range(ways)]
+    earlier, later = ([array], [array])
+    for _ in range(ways // 2):
+        earlier.append(lax.ppermute(earlier[-1], axis, up))
+    for _ in range((ways - 1) // 2):
+        later.append(lax.ppermute(later[-1], axis, down))
+    line = jnp.concatenate([*earlier[::-1], *later[1:]], axis=dim)
+    return jnp.roll(line, (lax.axis_index(axis) - ways // 2) * array.shape[dim], axis=dim)
 
 
 def owner_users(block_count, block_table, slot_count):
@@ -52,11 +65,7 @@
 ):
     row_count = cand_feats.shape[0]
     heads_here = w_out.shape[0] // DH
-    projected = jnp.dot(
-        lax.all_gather(cand_feats, "tp", axis=1, tiled=True),
-        w_in,
-        preferred_element_type=jnp.float32,
-    )
+    projected = jnp.dot(collect(cand_feats, "tp", 1), w_in, preferred_element_type=jnp.float32)
     activated = jax.nn.silu(projected).reshape(row_count, heads_here, 2, DH)
     queries = activated[:, :, 0, :].astype(jnp.bfloat16)
     gates = activated[:, :, 1, :].astype(jnp.bfloat16)

time: 249 us -> 249 us (level)
  starting transfers between devices: 18.2 us -> 27.5 us
  waiting for transfers between devices: 127 us -> 118 us
    all_gather x1 -> x0, waiting for transfers between devices: 32.6 us -> none  [per_device(): lax.all_gather(cand_feats, 'tp', axis=1, tiled=True)]
    ppermute x0 -> x7, waiting for transfers between devices: none -> 18.4 us  [the longest x4 18.3 us: collect(): earlier.append(lax.ppermute(earlier[-1], axis, up))]
    ppermute x0 -> x7, starting transfers between devices: none -> 9.37 us  [the longest x3 9.34 us: collect(): later.append(lax.ppermute(later[-1], axis, down))]
    all_to_all x1, waiting for transfers between devices: 55 us -> 60.6 us  [per_device(): lax.all_to_all(outgoing, 'user', split_axis=0, concat_axis=0, tiled=True)]
    unnamed x20 -> x37, local copies, waits for them, and re-layouts: 8.03 us -> 9.37 us
    unnamed x3 -> x2, waiting for transfers between devices: 35.8 us -> 35.2 us
  transfers between devices with their start and end apart: 4 -> 10, of which waited for: 4 -> 7; matrix products, arithmetic and copies ran while one was open for 3% -> 3% of each run, Pallas kernels for 0% -> 0%
where the time goes in v1:
time: 249 us; the launch traced here: 248 us
  waiting for transfers between devices  118 us (47%)
  local copies, waits for them, and re-layouts  45.9 us (18%)
  matrix products  41.5 us (17%)
  starting transfers between devices  27.5 us (11%)
  between operations  13.8 us (6%)
    all_to_all x1, waiting for transfers between devices, per_device(): lax.all_to_all(outgoing, 'user', split_axis=0, concat_axis=0, tiled=True)  60.6 us
    dot_general x2, matrix products, one_block(): jnp.einsum('hre,ehd->rhd', attn_weights, value_rows, preferred_element_ty...  38.8 us
    unnamed x2, waiting for transfers between devices  35.2 us
    ppermute x4, waiting for transfers between devices, collect(): earlier.append(lax.ppermute(earlier[-1], axis, up))  18.3 us
    mul x2, local copies, waits for them, and re-layouts, one_block(): same_user[:, :, None] * live_mask[None]  14.1 us
    all_to_all x1, starting transfers between devices, per_device(): lax.all_to_all(out_marks, 'user', split_axis=0, concat_axis=0, tiled=True)  11.6 us
    unnamed x37, local copies, waits for them, and re-layouts  9.37 us
    ppermute x3, starting transfers between devices, collect(): later.append(lax.ppermute(later[-1], axis, down))  9.34 us
  transfers between devices with their start and end apart: 10, of which 7 were waited for; matrix products, arithmetic and copies ran while one was open for 3% of the time, Pallas kernels for 0%

profile of v1, /device:TPU:2, one launch (start us, length us, event | category | flops | bytes accessed | tf_op | source)
XLA Modules:
  0.0 248.5 jit_solution(8455276338567292851)
XLA Ops:
  7.5 1.4 gather_fusion.1
  9.5 11.6 %all-to-all-start.1 = ((bf16[32,2,128]{2,1,0:T(2,128)(2,1)}), bf16[32,2,128]{2,1,0:T(2,128)(2,1)S(1)}, u32[]{:S(2)}, u32[]{:S(2)}) async-start(bf16[32,2,128]{2,1,0:T(2,128)(2,1)} %bitcast.14), calls=%async_computation.1 | async-start | bytes 32768 | tf_op jit(solution)/shard_map/all_to_all | solution.py:80
  21.1 5.0 %gather_fusion = bf16[64,128,256]{2,1,0:T(8,128)(2,1)} fusion(bf16[64,128,256]{2,1,0:T(8,128)(2,1)} %param.14, s32[1024]{0:T(1024)S(1)} %pad_clamp_fusion), kind=kCustom, calls=%fused_computation | custom fusion | bytes 8388864 | tf_op jit(solution)/shard_map/gather | solution.py:76
  26.1 3.5 %all-to-all-done.1 = bf16[32,2,128]{2,1,0:T(2,128)(2,1)S(1)} async-done(((bf16[32,2,128]{2,1,0:T(2,128)(2,1)}), bf16[32,2,128]{2,1,0:T(2,128)(2,1)S(1)}, u32[]{:S(2)}, u32[]{:S(2)}) %all-to-all-start.1) | async-done | bytes 16416 | tf_op jit(solution)/shard_map/all_to_all | solution.py:80
  29.5 6.5 %all-to-all-start = ((bf16[32,2,128,256]{3,2,1,0:T(8,128)(2,1)}), bf16[32,2,128,256]{3,2,1,0:T(8,128)(2,1)}, u32[]{:S(2)}, u32[]{:S(2)}) async-start(bf16[32,2,128,256]{3,2,1,0:T(8,128)(2,1)} %bitcast.91), calls=%async_computation | async-start | bytes 8388608 | tf_op jit(solution)/shard_map/all_to_all | solution.py:79
  36.2 7.0 %collective-permute-done = bf16[1024,128]{1,0:T(8,128)(2,1)S(1)} collective-permute-done((bf16[1024,128]{1,0:T(8,128)(2,1)S(1)}, bf16[1024,128]{1,0:T(8,128)(2,1)S(1)}, u32[]{:S(2)}, u32[]{:S(2)}) %collective-permute-start) | collective-permute-done | bytes 262176 | tf_op jit(solution)/shard_map/ppermute | solution.py:17
  43.2 3.0 %collective-permute-start.4 = (bf16[1024,128]{1,0:T(8,128)(2,1)S(1)}, bf16[1024,128]{1,0:T(8,128)(2,1)S(1)}, u32[]{:S(2)}, u32[]{:S(2)}) collective-permute-start(bf16[1024,128]{1,0:T(8,128)(2,1)S(1)} %copy-done.1), channel_id=1, source_target_pairs={{0,7},{1,0},{2,1},{3,2},{4,3},{5,4},{6,5},{7,6},{8,15},{9,8},{10,9... | collective-permute-start | bytes 786440 | tf_op jit(solution)/shard_map/ppermute | solution.py:19
  46.1 4.1 %collective-permute-done.1 = bf16[1024,128]{1,0:T(8,128)(2,1)S(1)} collective-permute-done((bf16[1024,128]{1,0:T(8,128)(2,1)S(1)}, bf16[1024,128]{1,0:T(8,128)(2,1)S(1)}, u32[]{:S(2)}, u32[]{:S(2)}) %collective-permute-start.1) | collective-permute-done | bytes 262176 | tf_op jit(solution)/shard_map/ppermute | solution.py:17
  50.2 3.3 %collective-permute-start.5 = (bf16[1024,128]{1,0:T(8,128)(2,1)S(1)}, bf16[1024,128]{1,0:T(8,128)(2,1)S(1)}, u32[]{:S(2)}, u32[]{:S(2)}) collective-permute-start(bf16[1024,128]{1,0:T(8,128)(2,1)S(1)} %collective-permute-done.4), channel_id=1, source_target_pairs={{0,7},{1,0},{2,1},{3,2},{4,3},{5,4},{6,5},{7,6},{8,15},{9,8},{10,9... | collective-permute-start | bytes 786440 | tf_op jit(solution)/shard_map/ppermute | solution.py:19
  53.5 3.7 %collective-permute-done.2 = bf16[1024,128]{1,0:T(8,128)(2,1)S(1)} collective-permute-done((bf16[1024,128]{1,0:T(8,128)(2,1)S(1)}, bf16[1024,128]{1,0:T(8,128)(2,1)S(1)}, u32[]{:S(2)}, u32[]{:S(2)}) %collective-permute-start.2) | collective-permute-done | bytes 262176 | tf_op jit(solution)/shard_map/ppermute | solution.py:17
  57.4 3.1 %collective-permute-start.6 = (bf16[1024,128]{1,0:T(8,128)(2,1)S(1)}, bf16[1024,128]{1,0:T(8,128)(2,1)S(1)}, u32[]{:S(2)}, u32[]{:S(2)}) collective-permute-start(bf16[1024,128]{1,0:T(8,128)(2,1)S(1)} %collective-permute-done.5), channel_id=1, source_target_pairs={{0,7},{1,0},{2,1},{3,2},{4,3},{5,4},{6,5},{7,6},{8,15},{9,8},{10,9... | collective-permute-start | bytes 786440 | tf_op jit(solution)/shard_map/ppermute | solution.py:19
  60.5 3.7 %collective-permute-done.3 = bf16[1024,128]{1,0:T(8,128)(2,1)S(1)} collective-permute-done((bf16[1024,128]{1,0:T(8,128)(2,1)S(1)}, bf16[1024,128]{1,0:T(8,128)(2,1)S(1)}, u32[]{:S(2)}, u32[]{:S(2)}) %collective-permute-start.3) | collective-permute-done | bytes 262176 | tf_op jit(solution)/shard_map/ppermute | solution.py:17
  68.3 60.6 %all-to-all-done = bf16[32,2,128,256]{3,2,1,0:T(8,128)(2,1)} async-done(((bf16[32,2,128,256]{3,2,1,0:T(8,128)(2,1)}), bf16[32,2,128,256]{3,2,1,0:T(8,128)(2,1)}, u32[]{:S(2)}, u32[]{:S(2)}) %all-to-all-start) | async-done | bytes 4194336 | tf_op jit(solution)/shard_map/all_to_all | solution.py:79
  128.9 7.0 %reshape.203 = bf16[8192,1,2,128]{3,2,0,1:T(2,128)(2,1)} reshape(bf16[32,2,128,256]{3,2,1,0:T(8,128)(2,1)} %all-to-all-done) | data formatting | bytes 8388608 | tf_op jit(solution)/shard_map/reshape | solution.py:37
  135.9 8.8 %fusion.34 = (bf16[8192,1,1,128]{3,2,0,1:T(2,128)(2,1)S(1)}, bf16[8192,1,1,128]{3,2,0,1:T(2,128)(2,1)S(1)}) fusion(bf16[8192,1,2,128]{3,2,0,1:T(2,128)(2,1)} %reshape.203), kind=kLoop, calls=%fused_computation.56 | loop fusion | bytes 8388608 | tf_op jit(solution)/shard_map/slice | solution.py:39
  144.6 1.9 copy_bitcast_fusion
  146.5 53.2 %while.10 = (s32[]{:T(128)}, f32[2,512,1,128]{3,1,2,0:T(8,128)S(1)}, bf16[2,512,1,128]{3,1,2,0:T(8,128)(2,1)S(1)}, bf16[8192,1,128]{2,0,1:T(8,128)(2,1)}, s32[2,...) while((s32[]{:T(128)}, ...), condition=%wide.region_2.3_spmd, body=%wide.region_1.2_spmd.sunk | while | flops 2181104128 | bytes 38444384 | solution.py:57
  146.7 7.0 %mul.131 = f32[512,64,128]{2,1,0:T(8,128)} broadcast(f32[512,64]{1,0:T(8,128)S(1)} %compare_convert_fusion.2), dimensions={0,1} | broadcast | bytes 16908288 | tf_op jit(solution)/shard_map/while/body/eval_jaxpr/mul | solution.py:48
  153.7 19.4 %fusion.44 = f32[2,512,1,128]{3,1,2,0:T(8,128)S(1)} fusion(f32[2,512,1,128]{3,1,2,0:T(8,128)S(1)} %get-tuple-element.151, s32[]{:T(128)} %get-tuple-element.150, bf16[8192,1,128]{2,0,1:T(8,128)(2,1)S(1)} %get-tuple-element.166, f32[64,8,64,128]{3,2,1,0:T(8,128)} %bitcast.90, f32[8192]{0:T(1024)S(1)} %bitcast.100, ...), kind=kOutput, calls=%fused_computation.9.clone.1 | convolution fusion | flops 2181038080 | bytes 21398528 | tf_op jit(solution)/shard_map/while/body/eval_jaxpr/hre,ehd->rhd/dot_general | solution.py:53
  173.2 7.0 %mul.131 = f32[512,64,128]{2,1,0:T(8,128)} broadcast(f32[512,64]{1,0:T(8,128)S(1)} %compare_convert_fusion.2), dimensions={0,1} | broadcast | bytes 16908288 | tf_op jit(solution)/shard_map/while/body/eval_jaxpr/mul | solution.py:48
  180.3 19.4 %fusion.44 = f32[2,512,1,128]{3,1,2,0:T(8,128)S(1)} fusion(f32[2,512,1,128]{3,1,2,0:T(8,128)S(1)} %get-tuple-element.151, s32[]{:T(128)} %get-tuple-element.150, bf16[8192,1,128]{2,0,1:T(8,128)(2,1)S(1)} %get-tuple-element.166, f32[64,8,64,128]{3,2,1,0:T(8,128)} %bitcast.90, f32[8192]{0:T(1024)S(1)} %bitcast.100, ...), kind=kOutput, calls=%fused_computation.9.clone.1 | convolution fusion | flops 2181038080 | bytes 21398528 | tf_op jit(solution)/shard_map/while/body/eval_jaxpr/hre,ehd->rhd/dot_general | solution.py:53
  200.1 1.8 convolution_convert_fusion
  201.9 2.6 %copy.25 = bf16[1024,1024]{0,1:T(8,128)(2,1)} copy(bf16[1024,1024]{1,0:T(8,128)(2,1)S(1)} %convolution_convert_fusion) | data formatting | bytes 4194304
  204.6 35.1 %reduce-scatter.4.cloned.1.call-done = bf16[128,1024]{1,0:T(8,128)(2,1)} async-done(((bf16[1024,1024]{1,0:T(8,128)(2,1)}), bf16[128,1024]{1,0:T(8,128)(2,1)}) %reduce-scatter.4.cloned.1.call-update) | async-done | bytes 262160
  (66 shorter events, 8.4 us)
Async XLA Ops:
  6.5 59.1 %copy-start = (bf16[1024,256]{1,0:T(8,128)(2,1)S(1)}, bf16[1024,256]{1,0:T(8,128)(2,1)}, u32[]{:S(2)}) copy-start(bf16[1024,256]{1,0:T(8,128)(2,1)} %param.12) | copy-start | bytes 1572868
  9.5 20.1 %all-to-all-start.1 = ((bf16[32,2,128]{2,1,0:T(2,128)(2,1)}), bf16[32,2,128]{2,1,0:T(2,128)(2,1)S(1)}, u32[]{:S(2)}, u32[]{:S(2)}) async-start(bf16[32,2,128]{2,1,0:T(2,128)(2,1)} %bitcast.14), calls=%async_computation.1 | async-start | bytes 32768 | tf_op jit(solution)/shard_map/all_to_all | solution.py:80
  29.5 6.6 %copy-start.1 = (bf16[1024,128]{1,0:T(8,128)(2,1)S(1)}, bf16[1024,128]{1,0:T(8,128)(2,1)}, u32[]{:S(2)}) copy-start(bf16[1024,128]{1,0:T(8,128)(2,1)} %param.11) | copy-start | bytes 786436
  29.5 20.6 %copy-start.7 = (s32[8]{0:T(128)S(1)}, s32[8]{0:T(128)}, u32[]{:S(2)}) copy-start(s32[8]{0:T(128)} %param.16) | copy-start | bytes 100
  29.5 27.6 %copy-start.5 = (s32[8,8]{1,0:T(8,128)S(1)}, s32[8,8]{1,0:T(8,128)}, u32[]{:S(2)}) copy-start(s32[8,8]{1,0:T(8,128)} %param.17) | copy-start | bytes 772
  29.5 27.8 %copy-start.6 = (s32[1024]{0:T(1024)S(1)}, s32[1024]{0:T(1024)}, u32[]{:S(2)}) copy-start(s32[1024]{0:T(1024)} %param.19) | copy-start | bytes 12292
  29.5 99.3 %all-to-all-start = ((bf16[32,2,128,256]{3,2,1,0:T(8,128)(2,1)}), bf16[32,2,128,256]{3,2,1,0:T(8,128)(2,1)}, u32[]{:S(2)}, u32[]{:S(2)}) async-start(bf16[32,2,128,256]{3,2,1,0:T(8,128)(2,1)} %bitcast.91), calls=%async_computation | async-start | bytes 8388608 | tf_op jit(solution)/shard_map/all_to_all | solution.py:79
  36.1 203.6 %reduce-scatter.4.cloned.1.call-start = ((), (), s32[]{:S(2)}) async-start(), calls=%async_computation.3 | async-start | bytes 2359296
  36.1 7.0 %collective-permute-start = (bf16[1024,128]{1,0:T(8,128)(2,1)S(1)}, bf16[1024,128]{1,0:T(8,128)(2,1)S(1)}, u32[]{:S(2)}, u32[]{:S(2)}) collective-permute-start(bf16[1024,128]{1,0:T(8,128)(2,1)S(1)} %copy-done.1), channel_id=1, source_target_pairs={{0,1},{1,2},{2,3},{3,4},{4,5},{5,6},{6,7},{7,0},{8,9},{9,10},{10,1... | collective-permute-start | bytes 786440 | tf_op jit(solution)/shard_map/ppermute | solution.py:17
  43.2 7.0 %collective-permute-start.1 = (bf16[1024,128]{1,0:T(8,128)(2,1)S(1)}, bf16[1024,128]{1,0:T(8,128)(2,1)S(1)}, u32[]{:S(2)}, u32[]{:S(2)}) collective-permute-start(bf16[1024,128]{1,0:T(8,128)(2,1)S(1)} %collective-permute-done), channel_id=1, source_target_pairs={{0,1},{1,2},{2,3},{3,4},{4,5},{5,6},{6,7},{7,0},{8,9},{9,10},{10,1... | collective-permute-start | bytes 786440 | tf_op jit(solution)/shard_map/ppermute | solution.py:17
  43.2 7.1 %collective-permute-start.4 = (bf16[1024,128]{1,0:T(8,128)(2,1)S(1)}, bf16[1024,128]{1,0:T(8,128)(2,1)S(1)}, u32[]{:S(2)}, u32[]{:S(2)}) collective-permute-start(bf16[1024,128]{1,0:T(8,128)(2,1)S(1)} %copy-done.1), channel_id=1, source_target_pairs={{0,7},{1,0},{2,1},{3,2},{4,3},{5,4},{6,5},{7,6},{8,15},{9,8},{10,9... | collective-permute-start | bytes 786440 | tf_op jit(solution)/shard_map/ppermute | solution.py:19
  50.2 7.0 %collective-permute-start.2 = (bf16[1024,128]{1,0:T(8,128)(2,1)S(1)}, bf16[1024,128]{1,0:T(8,128)(2,1)S(1)}, u32[]{:S(2)}, u32[]{:S(2)}) collective-permute-start(bf16[1024,128]{1,0:T(8,128)(2,1)S(1)} %collective-permute-done.1), channel_id=1, source_target_pairs={{0,1},{1,2},{2,3},{3,4},{4,5},{5,6},{6,7},{7,0},{8,9},{9,10},{10,1... | collective-permute-start | bytes 786440 | tf_op jit(solution)/shard_map/ppermute | solution.py:17
  50.2 7.2 %collective-permute-start.5 = (bf16[1024,128]{1,0:T(8,128)(2,1)S(1)}, bf16[1024,128]{1,0:T(8,128)(2,1)S(1)}, u32[]{:S(2)}, u32[]{:S(2)}) collective-permute-start(bf16[1024,128]{1,0:T(8,128)(2,1)S(1)} %collective-permute-done.4), channel_id=1, source_target_pairs={{0,7},{1,0},{2,1},{3,2},{4,3},{5,4},{6,5},{7,6},{8,15},{9,8},{10,9... | collective-permute-start | bytes 786440 | tf_op jit(solution)/shard_map/ppermute | solution.py:19
  57.2 7.0 %collective-permute-start.3 = (bf16[1024,128]{1,0:T(8,128)(2,1)S(1)}, bf16[1024,128]{1,0:T(8,128)(2,1)S(1)}, u32[]{:S(2)}, u32[]{:S(2)}) collective-permute-start(bf16[1024,128]{1,0:T(8,128)(2,1)S(1)} %collective-permute-done.2), channel_id=1, source_target_pairs={{0,1},{1,2},{2,3},{3,4},{4,5},{5,6},{6,7},{7,0},{8,9},{9,10},{10,1... | collective-permute-start | bytes 786440 | tf_op jit(solution)/shard_map/ppermute | solution.py:17
  57.4 7.4 %collective-permute-start.6 = (bf16[1024,128]{1,0:T(8,128)(2,1)S(1)}, bf16[1024,128]{1,0:T(8,128)(2,1)S(1)}, u32[]{:S(2)}, u32[]{:S(2)}) collective-permute-start(bf16[1024,128]{1,0:T(8,128)(2,1)S(1)} %collective-permute-done.5), channel_id=1, source_target_pairs={{0,7},{1,0},{2,1},{3,2},{4,3},{5,4},{6,5},{7,6},{8,15},{9,8},{10,9... | collective-permute-start | bytes 786440 | tf_op jit(solution)/shard_map/ppermute | solution.py:19
  66.6 0.8 copy-start.3
  144.6 1.9 copy-start.4
  201.9 38.9 %copy-start.2 = (bf16[1024,128]{1,0:T(8,128)(2,1)S(1)}, bf16[1024,128]{1,0:T(8,128)(2,1)}, u32[]{:S(2)}) copy-start(bf16[1024,128]{1,0:T(8,128)(2,1)} %param.11) | copy-start | bytes 786436
Sparse Core Ops, SparseCore 0:
  204.7 34.9 reduce-scatter.3
